TPU v7x, 128 devices: a whole 4x4x4 slice. The times are simulated.
128 devices in a mesh: row: 8 (over x_lo, z), col: 16 (over x_hi, y, core).
Axes of the slice: x: 4 (x_hi: 2, x_lo: 2; x = x_hi * 2 + x_lo), y: 4, z: 4, core: 2. Of those that a mesh axis runs over, the one named last changes fastest.
Arguments:
- start_basis: float32 [65536, 256], P(('row', 'col')), may hold values from -6 to 6
- affinity_tiles: bfloat16 [18432, 256, 256], P(('row', 'col')), may hold values from -0.046875 to 0.046875
- tile_rows: int32 [18432], P(('row', 'col')), may hold values from 0 to 15, as said below
- tile_cols: int32 [18432], P(('row', 'col')), may hold values from 0 to 31, as said below
- live_tiles: int32 [128], P(('row', 'col')), may hold values from 32 to 144, as said below
- filter_center: float32 [1], replicated, may hold values from -0.3 to 0.3
- filter_radius: float32 [1], replicated, may hold values from 0.6 to 1.2
Outputs:
- filtered: float32 [65536, 256], P(('row', 'col'))
Inputs may be any that keep to these rules, and one draw needn't show every extreme that they name: `tile_rows`: every value is a tile row of a device's row group; on every device the first 8 * 2 slots name each tile row once. `tile_cols`: every value is a tile column of a device's column group; on every device the first 16 * 2 slots name each tile column once. `live_tiles`: some device uses all 144 slots.
All inputs are finite; a program needn't handle non-finite values.
Results may differ from a plain program's by a relative error of at most 0.0003.
Values sent between devices are 32-bit elements; how exact they have to be, the bound alone decides.
A program may use at most 128 MiB of HBM per device.

v0:
```python
import jax
import jax.numpy as jnp
from jax import lax
from jax.sharding import PartitionSpec as P

BLK = 256


def apply_operator(piece, affinity_tiles, tile_rows, tile_cols, live_tiles):
    gathered = lax.all_gather(piece, "col", axis=0, tiled=True)
    width = piece.shape[1]
    col_span = gathered.shape[0] // BLK
    slot_total = affinity_tiles.shape[0]
    row_span = lax.axis_size("row") * piece.shape[0] // BLK
    blocks = gathered.reshape(col_span, BLK, width)
    group_count = 9
    group_size = slot_total // group_count
    tile_groups = affinity_tiles.reshape(group_count, group_size, BLK, BLK)
    row_groups = tile_rows.reshape(group_count, group_size)
    col_groups = tile_cols.reshape(group_count, group_size)
    slot_groups = jnp.arange(slot_total, dtype=jnp.int32).reshape(group_count, group_size)
    row_labels = jnp.arange(row_span, dtype=jnp.int32)

    def group_step(total, pieces):
        tiles_now, rows_now, cols_now, slots_now = pieces
        selected = jnp.take(blocks, cols_now, axis=0)
        products = jnp.einsum(
            "kab,kbj->kaj", tiles_now.astype(jnp.float32), selected, precision=lax.Precision.HIGHEST
        )
        live_mask = slots_now < live_tiles[0]
        row_select = ((rows_now[None, :] == row_labels[:, None]) & live_mask[None, :]).astype(
            jnp.float32
        )
        total = total + jnp.einsum(
            "ik,kaj->iaj", row_select, products, precision=lax.Precision.HIGHEST
        )
        return (total, None)

    initial = jnp.zeros((row_span, BLK, width), jnp.float32)
    partial_value, unused = lax.scan(
        group_step, initial, (tile_groups, row_groups, col_groups, slot_groups)
    )
    partial_value = partial_value.reshape(row_span * BLK, width)
    totals = lax.psum(partial_value, "row")
    return lax.dynamic_slice_in_dim(
        totals, lax.axis_index("row") * piece.shape[0], piece.shape[0], 0
    )


def local(
    start_basis, affinity_tiles, tile_rows, tile_cols, live_tiles, filter_center, filter_radius
):
    center = filter_center[0]
    radius = filter_radius[0]
    first = (
        apply_operator(start_basis, affinity_tiles, tile_rows, tile_cols, live_tiles)
        - center * start_basis
    ) / radius
    second = apply_operator(first, affinity_tiles, tile_rows, tile_cols, live_tiles)
    return 2.0 * (second - center * first) / radius - start_basis


def solution(mesh):
    return jax.shard_map(
        local,
        mesh=mesh,
        in_specs=(
            P(("row", "col"), None),
            P(("row", "col"), None, None),
            P(("row", "col")),
            P(("row", "col")),
            P(("row", "col")),
            P(),
            P(),
        ),
        out_specs=P(("row", "col"), None),
        check_vma=False,
    )
```

profile of v0, /device:TPU:0, one launch (start us, length us, event | category | flops | bytes accessed | tf_op | source)
XLA Modules:
  0.0 822.4 jit_solution(18367370499009058144)
XLA Ops:
  8.8 76.3 %all-gather.3.cloned.1.call-done = f32[8192,256]{1,0:T(8,128)} async-done(((f32[512,256]{1,0:T(8,128)}), f32[8192,256]{1,0:T(8,128)}) %all-gather.3.cloned.1.call-update) | async-done | bytes 8388624 | tf_op jit(solution)/shard_map/all_gather | solution.py:10
  85.2 217.1 %while.22 = (s32[]{:T(128)}, f32[16,256,256]{2,0,1:T(8,128)}, s32[9,16]{1,0:T(8,128)S(1)}, s32[9,16]{1,0:T(8,128)S(1)}, s32[1]{0:T(128)}, /*index=5*/bf16[9,16,2...) while((s32[]{:T(128)}, f32[16,256,256]{2,0,1:T(8,128)}, ...), condition=%wide.region_1.3_spmd.clone, body=%wide.region_0.2_spmd.clone.sunk | while | flops 3425699328 | bytes 31462588 | solution.py:40
  99.5 8.7 %select_add_fusion.4 = f32[16,256,256]{2,0,1:T(8,128)} fusion(f32[16,256,256]{2,0,1:T(8,128)} %get-tuple-element.313, f32[16,256,256]{2,1,0:T(8,128)} %fusion.58, pred[]{:T(512)S(6)} %compare.6, s32[16]{0:T(128)S(1)} %fusion.59, pred[16]{0:T(512)(128)(4,1)S(1)} %compare_bitcast_fusion.4), kind=kOutput, calls=%fused_computation.8.clone.1 | convolution fusion | flops 203424256 | bytes 12582993 | tf_op jit(solution)/shard_map/while/body/eval_jaxpr/ik,kaj->iaj/dot_general | solution.py:34
  122.4 10.0 %select_add_fusion.4 = f32[16,256,256]{2,0,1:T(8,128)} fusion(f32[16,256,256]{2,0,1:T(8,128)} %get-tuple-element.313, f32[16,256,256]{2,1,0:T(8,128)} %fusion.58, pred[]{:T(512)S(6)} %compare.6, s32[16]{0:T(128)S(1)} %fusion.59, pred[16]{0:T(512)(128)(4,1)S(1)} %compare_bitcast_fusion.4), kind=kOutput, calls=%fused_computation.8.clone.1 | convolution fusion | flops 203424256 | bytes 12582993 | tf_op jit(solution)/shard_map/while/body/eval_jaxpr/ik,kaj->iaj/dot_general | solution.py:34
  146.7 10.0 %select_add_fusion.4 = f32[16,256,256]{2,0,1:T(8,128)} fusion(f32[16,256,256]{2,0,1:T(8,128)} %get-tuple-element.313, f32[16,256,256]{2,1,0:T(8,128)} %fusion.58, pred[]{:T(512)S(6)} %compare.6, s32[16]{0:T(128)S(1)} %fusion.59, pred[16]{0:T(512)(128)(4,1)S(1)} %compare_bitcast_fusion.4), kind=kOutput, calls=%fused_computation.8.clone.1 | convolution fusion | flops 203424256 | bytes 12582993 | tf_op jit(solution)/shard_map/while/body/eval_jaxpr/ik,kaj->iaj/dot_general | solution.py:34
  171.0 10.0 %select_add_fusion.4 = f32[16,256,256]{2,0,1:T(8,128)} fusion(f32[16,256,256]{2,0,1:T(8,128)} %get-tuple-element.313, f32[16,256,256]{2,1,0:T(8,128)} %fusion.58, pred[]{:T(512)S(6)} %compare.6, s32[16]{0:T(128)S(1)} %fusion.59, pred[16]{0:T(512)(128)(4,1)S(1)} %compare_bitcast_fusion.4), kind=kOutput, calls=%fused_computation.8.clone.1 | convolution fusion | flops 203424256 | bytes 12582993 | tf_op jit(solution)/shard_map/while/body/eval_jaxpr/ik,kaj->iaj/dot_general | solution.py:34
  195.2 10.0 %select_add_fusion.4 = f32[16,256,256]{2,0,1:T(8,128)} fusion(f32[16,256,256]{2,0,1:T(8,128)} %get-tuple-element.313, f32[16,256,256]{2,1,0:T(8,128)} %fusion.58, pred[]{:T(512)S(6)} %compare.6, s32[16]{0:T(128)S(1)} %fusion.59, pred[16]{0:T(512)(128)(4,1)S(1)} %compare_bitcast_fusion.4), kind=kOutput, calls=%fused_computation.8.clone.1 | convolution fusion | flops 203424256 | bytes 12582993 | tf_op jit(solution)/shard_map/while/body/eval_jaxpr/ik,kaj->iaj/dot_general | solution.py:34
  219.5 10.0 %select_add_fusion.4 = f32[16,256,256]{2,0,1:T(8,128)} fusion(f32[16,256,256]{2,0,1:T(8,128)} %get-tuple-element.313, f32[16,256,256]{2,1,0:T(8,128)} %fusion.58, pred[]{:T(512)S(6)} %compare.6, s32[16]{0:T(128)S(1)} %fusion.59, pred[16]{0:T(512)(128)(4,1)S(1)} %compare_bitcast_fusion.4), kind=kOutput, calls=%fused_computation.8.clone.1 | convolution fusion | flops 203424256 | bytes 12582993 | tf_op jit(solution)/shard_map/while/body/eval_jaxpr/ik,kaj->iaj/dot_general | solution.py:34
  243.7 10.0 %select_add_fusion.4 = f32[16,256,256]{2,0,1:T(8,128)} fusion(f32[16,256,256]{2,0,1:T(8,128)} %get-tuple-element.313, f32[16,256,256]{2,1,0:T(8,128)} %fusion.58, pred[]{:T(512)S(6)} %compare.6, s32[16]{0:T(128)S(1)} %fusion.59, pred[16]{0:T(512)(128)(4,1)S(1)} %compare_bitcast_fusion.4), kind=kOutput, calls=%fused_computation.8.clone.1 | convolution fusion | flops 203424256 | bytes 12582993 | tf_op jit(solution)/shard_map/while/body/eval_jaxpr/ik,kaj->iaj/dot_general | solution.py:34
  268.0 10.0 %select_add_fusion.4 = f32[16,256,256]{2,0,1:T(8,128)} fusion(f32[16,256,256]{2,0,1:T(8,128)} %get-tuple-element.313, f32[16,256,256]{2,1,0:T(8,128)} %fusion.58, pred[]{:T(512)S(6)} %compare.6, s32[16]{0:T(128)S(1)} %fusion.59, pred[16]{0:T(512)(128)(4,1)S(1)} %compare_bitcast_fusion.4), kind=kOutput, calls=%fused_computation.8.clone.1 | convolution fusion | flops 203424256 | bytes 12582993 | tf_op jit(solution)/shard_map/while/body/eval_jaxpr/ik,kaj->iaj/dot_general | solution.py:34
  292.3 10.0 %select_add_fusion.4 = f32[16,256,256]{2,0,1:T(8,128)} fusion(f32[16,256,256]{2,0,1:T(8,128)} %get-tuple-element.313, f32[16,256,256]{2,1,0:T(8,128)} %fusion.58, pred[]{:T(512)S(6)} %compare.6, s32[16]{0:T(128)S(1)} %fusion.59, pred[16]{0:T(512)(128)(4,1)S(1)} %compare_bitcast_fusion.4), kind=kOutput, calls=%fused_computation.8.clone.1 | convolution fusion | flops 203424256 | bytes 12582993 | tf_op jit(solution)/shard_map/while/body/eval_jaxpr/ik,kaj->iaj/dot_general | solution.py:34
  310.3 102.1 %all-reduce.3.cloned.1.call-done = f32[4096,256]{1,0:T(8,128)} async-done(((f32[4096,256]{1,0:T(8,128)}), f32[4096,256]{1,0:T(8,128)}) %all-reduce.3.cloned.1.call-update) | async-done | bytes 4194320 | tf_op jit(solution)/shard_map/psum | solution.py:44
  414.6 71.9 %all-gather.5.cloned.1.call-done = f32[8192,256]{1,0:T(8,128)} async-done(((f32[512,256]{1,0:T(8,128)}), f32[8192,256]{1,0:T(8,128)}) %all-gather.5.cloned.1.call-update) | async-done | bytes 8388624 | tf_op jit(solution)/shard_map/all_gather | solution.py:10
  486.5 217.1 %while.23 = (s32[]{:T(128)}, f32[16,256,256]{2,0,1:T(8,128)}, s32[9,16]{1,0:T(8,128)S(1)}, s32[9,16]{1,0:T(8,128)S(1)}, s32[1]{0:T(128)}, /*index=5*/bf16[9,16,2...) while((s32[]{:T(128)}, f32[16,256,256]{2,0,1:T(8,128)}, ...), condition=%wide.region_4.6_spmd.clone, body=%wide.region_3.5_spmd.clone.sunk | while | flops 3425699328 | bytes 31462588 | solution.py:40
  500.8 8.7 %select_add_fusion.5 = f32[16,256,256]{2,0,1:T(8,128)} fusion(f32[16,256,256]{2,0,1:T(8,128)} %get-tuple-element.343, f32[16,256,256]{2,1,0:T(8,128)} %fusion.64, pred[]{:T(512)S(6)} %compare.7, s32[16]{0:T(128)S(1)} %fusion.65, pred[16]{0:T(512)(128)(4,1)S(1)} %compare_bitcast_fusion.5), kind=kOutput, calls=%fused_computation.33.clone.1 | convolution fusion | flops 203424256 | bytes 12582993 | tf_op jit(solution)/shard_map/while/body/eval_jaxpr/ik,kaj->iaj/dot_general | solution.py:34
  523.7 10.0 %select_add_fusion.5 = f32[16,256,256]{2,0,1:T(8,128)} fusion(f32[16,256,256]{2,0,1:T(8,128)} %get-tuple-element.343, f32[16,256,256]{2,1,0:T(8,128)} %fusion.64, pred[]{:T(512)S(6)} %compare.7, s32[16]{0:T(128)S(1)} %fusion.65, pred[16]{0:T(512)(128)(4,1)S(1)} %compare_bitcast_fusion.5), kind=kOutput, calls=%fused_computation.33.clone.1 | convolution fusion | flops 203424256 | bytes 12582993 | tf_op jit(solution)/shard_map/while/body/eval_jaxpr/ik,kaj->iaj/dot_general | solution.py:34
  548.0 10.0 %select_add_fusion.5 = f32[16,256,256]{2,0,1:T(8,128)} fusion(f32[16,256,256]{2,0,1:T(8,128)} %get-tuple-element.343, f32[16,256,256]{2,1,0:T(8,128)} %fusion.64, pred[]{:T(512)S(6)} %compare.7, s32[16]{0:T(128)S(1)} %fusion.65, pred[16]{0:T(512)(128)(4,1)S(1)} %compare_bitcast_fusion.5), kind=kOutput, calls=%fused_computation.33.clone.1 | convolution fusion | flops 203424256 | bytes 12582993 | tf_op jit(solution)/shard_map/while/body/eval_jaxpr/ik,kaj->iaj/dot_general | solution.py:34
  572.3 10.0 %select_add_fusion.5 = f32[16,256,256]{2,0,1:T(8,128)} fusion(f32[16,256,256]{2,0,1:T(8,128)} %get-tuple-element.343, f32[16,256,256]{2,1,0:T(8,128)} %fusion.64, pred[]{:T(512)S(6)} %compare.7, s32[16]{0:T(128)S(1)} %fusion.65, pred[16]{0:T(512)(128)(4,1)S(1)} %compare_bitcast_fusion.5), kind=kOutput, calls=%fused_computation.33.clone.1 | convolution fusion | flops 203424256 | bytes 12582993 | tf_op jit(solution)/shard_map/while/body/eval_jaxpr/ik,kaj->iaj/dot_general | solution.py:34
  596.5 10.0 %select_add_fusion.5 = f32[16,256,256]{2,0,1:T(8,128)} fusion(f32[16,256,256]{2,0,1:T(8,128)} %get-tuple-element.343, f32[16,256,256]{2,1,0:T(8,128)} %fusion.64, pred[]{:T(512)S(6)} %compare.7, s32[16]{0:T(128)S(1)} %fusion.65, pred[16]{0:T(512)(128)(4,1)S(1)} %compare_bitcast_fusion.5), kind=kOutput, calls=%fused_computation.33.clone.1 | convolution fusion | flops 203424256 | bytes 12582993 | tf_op jit(solution)/shard_map/while/body/eval_jaxpr/ik,kaj->iaj/dot_general | solution.py:34
  620.8 10.0 %select_add_fusion.5 = f32[16,256,256]{2,0,1:T(8,128)} fusion(f32[16,256,256]{2,0,1:T(8,128)} %get-tuple-element.343, f32[16,256,256]{2,1,0:T(8,128)} %fusion.64, pred[]{:T(512)S(6)} %compare.7, s32[16]{0:T(128)S(1)} %fusion.65, pred[16]{0:T(512)(128)(4,1)S(1)} %compare_bitcast_fusion.5), kind=kOutput, calls=%fused_computation.33.clone.1 | convolution fusion | flops 203424256 | bytes 12582993 | tf_op jit(solution)/shard_map/while/body/eval_jaxpr/ik,kaj->iaj/dot_general | solution.py:34
  645.1 10.0 %select_add_fusion.5 = f32[16,256,256]{2,0,1:T(8,128)} fusion(f32[16,256,256]{2,0,1:T(8,128)} %get-tuple-element.343, f32[16,256,256]{2,1,0:T(8,128)} %fusion.64, pred[]{:T(512)S(6)} %compare.7, s32[16]{0:T(128)S(1)} %fusion.65, pred[16]{0:T(512)(128)(4,1)S(1)} %compare_bitcast_fusion.5), kind=kOutput, calls=%fused_computation.33.clone.1 | convolution fusion | flops 203424256 | bytes 12582993 | tf_op jit(solution)/shard_map/while/body/eval_jaxpr/ik,kaj->iaj/dot_general | solution.py:34
  669.3 10.0 %select_add_fusion.5 = f32[16,256,256]{2,0,1:T(8,128)} fusion(f32[16,256,256]{2,0,1:T(8,128)} %get-tuple-element.343, f32[16,256,256]{2,1,0:T(8,128)} %fusion.64, pred[]{:T(512)S(6)} %compare.7, s32[16]{0:T(128)S(1)} %fusion.65, pred[16]{0:T(512)(128)(4,1)S(1)} %compare_bitcast_fusion.5), kind=kOutput, calls=%fused_computation.33.clone.1 | convolution fusion | flops 203424256 | bytes 12582993 | tf_op jit(solution)/shard_map/while/body/eval_jaxpr/ik,kaj->iaj/dot_general | solution.py:34
  693.6 10.0 %select_add_fusion.5 = f32[16,256,256]{2,0,1:T(8,128)} fusion(f32[16,256,256]{2,0,1:T(8,128)} %get-tuple-element.343, f32[16,256,256]{2,1,0:T(8,128)} %fusion.64, pred[]{:T(512)S(6)} %compare.7, s32[16]{0:T(128)S(1)} %fusion.65, pred[16]{0:T(512)(128)(4,1)S(1)} %compare_bitcast_fusion.5), kind=kOutput, calls=%fused_computation.33.clone.1 | convolution fusion | flops 203424256 | bytes 12582993 | tf_op jit(solution)/shard_map/while/body/eval_jaxpr/ik,kaj->iaj/dot_general | solution.py:34
  710.2 103.5 %all-reduce.5.cloned.1.call-done = f32[4096,256]{1,0:T(8,128)} async-done(((f32[4096,256]{1,0:T(8,128)}), f32[4096,256]{1,0:T(8,128)}) %all-reduce.5.cloned.1.call-update) | async-done | bytes 4194320 | tf_op jit(solution)/shard_map/psum | solution.py:44
  (127 shorter events, 276.2 us)
Async XLA Ops:
  6.5 78.6 %all-gather.3.cloned.1.call-start = ((), (), s32[]{:S(2)}) async-start(), calls=%async_computation | async-start | bytes 8912896 | tf_op jit(solution)/shard_map/all_gather | solution.py:10
  7.3 405.1 %all-reduce.3.cloned.1.call-start = ((), (), s32[]{:S(2)}) async-start(), calls=%async_computation.1 | async-start | bytes 8388608 | tf_op jit(solution)/shard_map/psum | solution.py:44
  308.8 103.6 %copy-start = (f32[512,256]{1,0:T(8,128)S(1)}, f32[512,256]{1,0:T(8,128)}, u32[]{:S(2)}) copy-start(f32[512,256]{1,0:T(8,128)} %param.13) | copy-start | bytes 1572868
  308.9 177.6 %all-gather.5.cloned.1.call-start = ((), (), s32[]{:S(2)}) async-start(), calls=%async_computation.2 | async-start | bytes 8912896 | tf_op jit(solution)/shard_map/all_gather | solution.py:10
  414.3 399.4 %all-reduce.5.cloned.1.call-start = ((), (), s32[]{:S(2)}) async-start(), calls=%async_computation.3 | async-start | bytes 8388608 | tf_op jit(solution)/shard_map/psum | solution.py:44
Sparse Core Ops, SparseCore 0:
  9.8 75.3 all-gather.2
  309.0 103.3 all-reduce.2
  414.9 71.5 all-gather.4
  710.3 103.3 all-reduce.4
where the time goes:
time: 824 us; the launch traced here: 822 us
  waiting for transfers between devices  355 us (43%)
  matrix products  311 us (38%)
  local copies, waits for them, and re-layouts  125 us (15%)
  other arithmetic  16.2 us (2%)
  between operations  14.5 us (2%)
    psum x2, waiting for transfers between devices, apply_operator(): totals = lax.psum(partial_value, 'row')  206 us
    dot_general x18, matrix products, group_step(): jnp.einsum('ik,kaj->iaj', row_select, products, precision=lax.Precision.H...  177 us
    all_gather x2, waiting for transfers between devices, apply_operator(): gathered = lax.all_gather(piece, 'col', axis=0, tiled=True)  148 us
    dot_general x18, matrix products, group_step(): jnp.einsum('kab,kbj->kaj', tiles_now.astype(jnp.float32), selected, preci...  134 us
    gather x18, local copies, waits for them, and re-layouts, group_step(): selected = jnp.take(blocks, cols_now, axis=0)  111 us
  transfers between devices with their start and end apart: 4, of which 4 were waited for; matrix products, arithmetic and copies ran while one was open for 0% of the time, Pallas kernels for 0%

commit v1 on v0

v1 whole, which is shorter than its diff:
```python
import functools

import jax
import jax.numpy as jnp
from jax import lax
from jax.experimental import pallas as pl
from jax.experimental.pallas import tpu as pltpu
from jax.sharding import PartitionSpec as P

MESH = pl.DeviceIdType.MESH
F32 = jnp.float32
BF16 = jnp.bfloat16
BLK = 256
NT = 144
PIECE = 512
K = 256
NCH = 4
QC = K // NCH
HC = QC // 2
STAGES = 2 * NCH
GROUPS = 80
UNROLL = 16
PARTS = 8
SLOTS = 4


def filter_kernel(
    x_ref, t_hbm, rows_ref, cols_ref, live_ref, cen_ref, rad_ref, o_ref,
    tiles, gath, vals, sums, part, got_a, got_n, got_x, x_t, o_t, ivec, idx,
    t_sem, i_sem, g_send, g_recv, r_send, r_recv,
):
    row = lax.axis_index("row")
    col = lax.axis_index("col")
    xl, z = row // 4, row % 4
    xh, y, core = col // 8, (col // 2) % 4, col % 2

    def dev(xh_, xl_, y_, z_, core_):
        return (xl_ * 4 + z_, xh_ * 8 + y_ * 2 + core_)

    up, down = dev(xh, xl, (y + 1) % 4, z, core), dev(xh, xl, (y + 3) % 4, z, core)
    zup, zdown = dev(xh, xl, y, (z + 1) % 4, core), dev(xh, xl, y, (z + 3) % 4, core)
    sib = dev(xh, xl, y, z, 1 - core)
    far = dev(1 - xh, xl, y, z, core)
    near = dev(xh, 1 - xl, y, z, core)

    per = NT // PARTS

    def tile_copy(i):
        span = pl.ds(i * per, per)
        return pltpu.make_async_copy(t_hbm.at[span], tiles.at[span], t_sem.at[i])

    for i in range(PARTS):
        tile_copy(i).start()

    def send(src, dst, ssem, rsem, to):
        pltpu.make_async_remote_copy(
            src_ref=src, dst_ref=dst, send_sem=ssem, recv_sem=rsem, device_id=to, device_id_type=MESH
        ).start()

    def wait_recv(ref, sem):
        pltpu.make_async_remote_copy(
            src_ref=ref, dst_ref=ref, send_sem=g_send, recv_sem=sem, device_id=sib, device_id_type=MESH
        ).wait_recv()

    def wait_send(ref, sem):
        pltpu.make_async_remote_copy(
            src_ref=ref, dst_ref=ref, send_sem=sem, recv_sem=g_recv.at[0, 0], device_id=sib, device_id_type=MESH
        ).wait_send()

    def piece(k, core_, xh_, y_):
        return gath.at[k * 16 + core_ * 8 + xh_ * 4 + y_]

    lo_half, hi_half = pl.ds(0, HC), pl.ds(HC, HC)
    S_L, S_R, S_X, S_Y2, S_XL, S_XR, S_X2, S_SIB = range(8)

    def to_sib(k, ref):
        send(ref, ref, g_send, g_recv.at[k, S_SIB], sib)

    def gather_own(k):
        own = piece(k, core, xh, y)
        send(own, own, g_send, g_recv.at[k, S_L], up)
        send(own, own, g_send, g_recv.at[k, S_R], down)
        send(own, own, g_send, g_recv.at[k, S_X], far)
        to_sib(k, own)

    def gather_one(k):
        left, right = piece(k, core, xh, (y + 3) % 4), piece(k, core, xh, (y + 1) % 4)
        opp = piece(k, core, 1 - xh, y)
        wait_recv(opp, g_recv.at[k, S_X])
        send(opp, opp, g_send, g_recv.at[k, S_XL], up)
        send(opp, opp, g_send, g_recv.at[k, S_XR], down)
        wait_recv(left, g_recv.at[k, S_L])
        send(left.at[lo_half], left.at[lo_half], g_send, g_recv.at[k, S_Y2], up)
        wait_recv(right, g_recv.at[k, S_R])
        send(right.at[hi_half], right.at[hi_half], g_send, g_recv.at[k, S_Y2], down)
        to_sib(k, opp)
        to_sib(k, left)
        to_sib(k, right)

    def gather_two(k):
        left, right = piece(k, core, 1 - xh, (y + 3) % 4), piece(k, core, 1 - xh, (y + 1) % 4)
        wait_recv(left, g_recv.at[k, S_XL])
        send(left.at[lo_half], left.at[lo_half], g_send, g_recv.at[k, S_X2], up)
        wait_recv(right, g_recv.at[k, S_XR])
        send(right.at[hi_half], right.at[hi_half], g_send, g_recv.at[k, S_X2], down)
        to_sib(k, left)
        to_sib(k, right)

    def gather_end(k):
        mine, other = piece(k, core, xh, (y + 2) % 4), piece(k, core, 1 - xh, (y + 2) % 4)
        wait_recv(mine, g_recv.at[k, S_Y2])
        to_sib(k, mine)
        wait_recv(other, g_recv.at[k, S_X2])
        to_sib(k, other)
        wait_recv(gath.at[pl.ds(k * 16 + (1 - core) * 8, 8)], g_recv.at[k, S_SIB])
        for core_ in range(2):
            for m in range(8):
                block = gath[k * 16 + core_ * 8 + m]
                high = block.astype(BF16)
                low = (block - high.astype(F32)).astype(BF16)
                for t in range(2):
                    j = (2 * m + core_) * 2 + t
                    vals[j, 0:QC] = high[:, t * BLK : (t + 1) * BLK]
                    vals[j, QC : 2 * QC] = low[:, t * BLK : (t + 1) * BLK]

    R_A, R_N, R_X = 0, 2, 4
    sides = (1 - xl, xl)

    def part_at(k, xl_, z_):
        return part.at[(k % SLOTS) * 8 + xl_ * 4 + z_]

    def multiply(k):
        @pl.loop(0, GROUPS // UNROLL)
        def _(i):
            for u in range(UNROLL):
                g = i * UNROLL + u
                p0, p1 = idx[0, 2 * g], idx[0, 2 * g + 1]
                c0, c1 = idx[1, 2 * g], idx[1, 2 * g + 1]
                d = jnp.dot(vals[c0], tiles[p0], preferred_element_type=F32) + jnp.dot(
                    vals[c1], tiles[p1], preferred_element_type=F32
                )
                keep = idx[2, g].astype(F32)
                sums[g + 1] = sums[g] * keep + (d[:QC] + d[QC:])

        @pl.when(k >= SLOTS)
        def _():
            wait_send(part.at[pl.ds(0, 7)], r_send.at[k % SLOTS])

        for i in range(16):
            part[(k % SLOTS) * 8 + i // 2, :, (i % 2) * BLK : (i % 2 + 1) * BLK] = sums[idx[3, i]]
        ssem = r_send.at[k % SLOTS]
        for g in range(2):
            a = part_at(k, sides[g], (z + 2) % 4)
            send(a.at[lo_half], got_a.at[k * 4 + g * 2 + 0], ssem, r_recv.at[k, R_A + g], zup)
            send(a.at[hi_half], got_a.at[k * 4 + g * 2 + 1], ssem, r_recv.at[k, R_A + g], zdown)
        send_plain(k, 0)

    def send_plain(k, g):
        ssem = r_send.at[k % SLOTS]
        n_up, n_down = part_at(k, sides[g], (z + 1) % 4), part_at(k, sides[g], (z + 3) % 4)
        send(n_up.at[hi_half], got_n.at[k * 4 + g * 2 + 0, hi_half], ssem, r_recv.at[k, R_N + g], zup)
        send(n_down.at[lo_half], got_n.at[k * 4 + g * 2 + 1, lo_half], ssem, r_recv.at[k, R_N + g], zdown)

    def reduce_one(k):
        ssem = r_send.at[k % SLOTS]
        for g in range(2):
            wait_recv(got_a.at[pl.ds(k * 4 + g * 2, 2)], r_recv.at[k, R_A + g])
            n_up, n_down = part_at(k, sides[g], (z + 1) % 4), part_at(k, sides[g], (z + 3) % 4)
            n_up[0:HC] = n_up[0:HC] + got_a[k * 4 + g * 2 + 0]
            n_down[HC:QC] = n_down[HC:QC] + got_a[k * 4 + g * 2 + 1]
            send(n_up.at[lo_half], got_n.at[k * 4 + g * 2 + 0, lo_half], ssem, r_recv.at[k, R_N + g], zup)
            send(n_down.at[hi_half], got_n.at[k * 4 + g * 2 + 1, hi_half], ssem, r_recv.at[k, R_N + g], zdown)
            if g == 0:
                send_plain(k, 1)

    def reduce_two(k):
        wait_recv(got_n.at[pl.ds(k * 4, 2)], r_recv.at[k, R_N])
        mine = part_at(k, 1 - xl, z)
        mine[...] = mine[...] + got_n[k * 4] + got_n[k * 4 + 1]
        send(mine, got_x.at[k], r_send.at[k % SLOTS], r_recv.at[k, R_X], near)

    def reduce_end(k):
        wait_recv(got_n.at[pl.ds(k * 4 + 2, 2)], r_recv.at[k, R_N + 1])
        wait_recv(got_x.at[k], r_recv.at[k, R_X])
        mine = part_at(k, xl, z)
        total = mine[...] + got_n[k * 4 + 2] + got_n[k * 4 + 3] + got_x[k]
        center, radius = cen_ref[0], rad_ref[0]
        cols_at = pl.ds(pl.multiple_of((k % NCH) * QC, QC), QC)
        start = x_t[cols_at]

        @pl.when(k < NCH)
        def _():
            gath[(k + NCH) * 16 + core * 8 + xh * 4 + y] = (total - center * start) / radius

        @pl.when(k >= NCH)
        def _():
            first = gath[k * 16 + core * 8 + xh * 4 + y]
            o_t[cols_at] = 2.0 * (total - center * first) / radius - start

    x_t[...] = x_ref[...].T
    for j in range(NCH):
        gath[j * 16 + core * 8 + xh * 4 + y] = x_t[j * QC : (j + 1) * QC]

    barrier = pltpu.get_barrier_semaphore()
    others = (up, down, zup, zdown, sib, far, near)
    for other in others:
        pl.semaphore_signal(barrier, inc=1, device_id=other, device_id_type=MESH)
    pl.semaphore_wait(barrier, len(others))

    gather_own(0)

    ivec[...] = jnp.full(ivec.shape, 99, jnp.int32)
    ivec[0:1, 0:NT] = rows_ref[...]
    ivec[1:2, 0:NT] = cols_ref[...]
    lanes = lax.broadcasted_iota(jnp.int32, (1, 256), 1)
    row_of = jnp.where(lanes < live_ref[0], ivec[0:1], 99)
    row_l = jnp.broadcast_to(row_of, (256, 256))
    row_s = row_l.T
    col_s = jnp.broadcast_to(ivec[1:2], (256, 256)).T
    li = lax.broadcasted_iota(jnp.int32, (256, 256), 1)
    si = lax.broadcasted_iota(jnp.int32, (256, 256), 0)

    def count(mask, value=1, axis=1):
        return jnp.sum(jnp.where(mask, value, 0), axis=axis, keepdims=True)

    within = count((row_l == row_s) & (li < si))
    pairs = (count(row_s == li, axis=0) + 1) >> 1
    before = count(li < row_s, pairs)
    pairs_s = count(li == row_s, pairs)
    live = row_s < 16
    place = live & (2 * before + within == li)
    leads = live & (within == 0)
    ivec[0:1] = count(place, si, 0)
    ivec[1:2] = count(place, col_s - 32, 0) + 32
    ivec[2:3] = 1 - count(leads & (before == li), 1, 0)
    ivec[3:4] = count(leads & (row_s <= li), pairs_s, 0)
    to_smem = pltpu.make_async_copy(ivec, idx, i_sem)
    to_smem.start()

    def turn(i):
        tile_copy(i).wait()

        @pl.loop(0, per)
        def _(s):
            tiles[i * per + s] = tiles[i * per + s].T

    vals[32] = jnp.zeros((2 * QC, BLK), BF16)
    sums[0] = jnp.zeros((QC, BLK), F32)
    for i in range(PARTS // 2):
        turn(i)
    gather_one(0)
    gather_own(1)
    for i in range(PARTS // 2, PARTS):
        turn(i)
    gather_two(0)
    to_smem.wait()

    @pl.loop(1, STAGES + 3)
    def _(k):
        @pl.when(k <= STAGES)
        def _():
            gather_end(k - 1)

        @pl.when(k >= 3)
        def _():
            reduce_end(k - 3)

        @pl.when((k >= 2) & (k < STAGES + 2))
        def _():
            reduce_one(k - 2)

        @pl.when(k < STAGES)
        def _():
            gather_one(k)

        @pl.when(k < STAGES - 1)
        def _():
            gather_own(k + 1)

        @pl.when(k <= STAGES)
        def _():
            multiply(k - 1)

        @pl.when(k < STAGES)
        def _():
            gather_two(k)

        @pl.when((k >= 2) & (k < STAGES + 2))
        def _():
            reduce_two(k - 2)

    wait_send(gath.at[pl.ds(0, 15 * STAGES)], g_send)
    for s in range(SLOTS):
        wait_send(part.at[pl.ds(0, 7)], r_send.at[s])
    o_ref[...] = o_t[...].T


def local(start_basis, affinity_tiles, tile_rows, tile_cols, live_tiles, filter_center, filter_radius):
    vmem = pl.BlockSpec(memory_space=pltpu.VMEM)
    smem = pl.BlockSpec(memory_space=pltpu.SMEM)
    return pl.pallas_call(
        filter_kernel,
        name="chebyshev_filter",
        out_shape=jax.ShapeDtypeStruct((PIECE, K), F32),
        in_specs=[vmem, pl.BlockSpec(memory_space=pl.ANY), vmem, vmem, smem, smem, smem],
        out_specs=vmem,
        scratch_shapes=[
            pltpu.VMEM((NT, BLK, BLK), BF16),
            pltpu.VMEM((STAGES * 16, QC, PIECE), F32),
            pltpu.VMEM((33, 2 * QC, BLK), BF16),
            pltpu.VMEM((GROUPS + 1, QC, BLK), F32),
            pltpu.VMEM((SLOTS * 8, QC, PIECE), F32),
            pltpu.VMEM((STAGES * 4, HC, PIECE), F32),
            pltpu.VMEM((STAGES * 4, QC, PIECE), F32),
            pltpu.VMEM((STAGES, QC, PIECE), F32),
            pltpu.VMEM((K, PIECE), F32),
            pltpu.VMEM((K, PIECE), F32),
            pltpu.VMEM((8, 256), jnp.int32),
            pltpu.SMEM((8, 256), jnp.int32),
            pltpu.SemaphoreType.DMA((PARTS,)),
            pltpu.SemaphoreType.DMA,
            pltpu.SemaphoreType.DMA,
            pltpu.SemaphoreType.DMA((STAGES, 8)),
            pltpu.SemaphoreType.DMA((SLOTS,)),
            pltpu.SemaphoreType.DMA((STAGES, 5)),
        ],
        compiler_params=pltpu.CompilerParams(
            collective_id=0, has_side_effects=True, vmem_limit_bytes=60 * 2**20
        ),
        cost_estimate=pl.CostEstimate(
            flops=4 * NT * BLK * BLK * K * 2, bytes_accessed=NT * BLK * BLK * 2, transcendentals=0
        ),
    )(
        start_basis, affinity_tiles, tile_rows.reshape(1, NT), tile_cols.reshape(1, NT),
        live_tiles, filter_center, filter_radius,
    )


def solution(mesh):
    return jax.shard_map(
        local,
        mesh=mesh,
        in_specs=(
            P(("row", "col"), None),
            P(("row", "col"), None, None),
            P(("row", "col")),
            P(("row", "col")),
            P(("row", "col")),
            P(),
            P(),
        ),
        out_specs=P(("row", "col"), None),
        check_vma=False,
    )
```

time: 824 us -> 136 us (0.17)
  waiting for transfers between devices: 355 us -> 0 us
  matrix products: 311 us -> 0 us
  Pallas kernels: 0 us -> 131 us
  local copies, waits for them, and re-layouts: 125 us -> 1.87 us
  other arithmetic: 16.2 us -> 0 us
  between operations: 14.5 us -> 1.95 us
    dot_general x36 -> x0, matrix products: 311 us -> none  [the longest x18 177 us: group_step(): jnp.einsum('ik,kaj->iaj', row_select, products, precision=lax.Precision.H...]
    psum x2 -> x0, waiting for transfers between devices: 206 us -> none  [apply_operator(): totals = lax.psum(partial_value, 'row')]
    all_gather x2 -> x0, waiting for transfers between devices: 148 us -> none  [apply_operator(): gathered = lax.all_gather(piece, 'col', axis=0, tiled=True)]
    pallas_call x0 -> x1, Pallas kernels: none -> 131 us  [local(): pl.pallas_call(filter_kernel, name='chebyshev_filter', out_shape=jax.Shap...]
    gather x18 -> x0, local copies, waits for them, and re-layouts: 111 us -> none  [group_step(): selected = jnp.take(blocks, cols_now, axis=0)]
    while x2 -> x0, local copies, waits for them, and re-layouts: 13.2 us -> none  [apply_operator(): lax.scan(group_step, initial, (tile_groups, row_groups, col_groups, slot_...]
    and x36 -> x0, other arithmetic: 12 us -> none  [the longest x18 11.8 us: group_step(): (rows_now[None, :] == row_labels[:, None]) & live_mask[None, :]]
  transfers between devices with their start and end apart: 4 -> 0, of which waited for: 4 -> 0; matrix products, arithmetic and copies ran while one was open for 0% -> 0% of each run, Pallas kernels for 0% -> 0%
where the time goes in v1:
time: 136 us; the launch traced here: 135 us
  Pallas kernels  131 us (96%)
  between operations  1.95 us (1%)
  local copies, waits for them, and re-layouts  1.87 us (1%)
    pallas_call x1, Pallas kernels, local(): pl.pallas_call(filter_kernel, name='chebyshev_filter', out_shape=jax.Shap...  131 us

profile of v1, /device:TPU:0, one launch (start us, length us, event | category | flops | bytes accessed | tf_op | source)
XLA Modules:
  0.0 135.3 jit_solution(16137596595947442015)
XLA Ops:
  1.9 131.5 %chebyshev_filter.1 = f32[512,256]{1,0:T(8,128)} custom-call(f32[512,256]{1,0:T(8,128)} %x_ref.1, bf16[144,256,256]{2,1,0:T(8,128)(2,1)} %t_hbm.1, s32[1,144]{1,0:T(1,128)} %bitcast.2, s32[1,144]{1,0:T(1,128)} %bitcast.3, s32[1]{0:T(128)S(6)} %copy.9.live_ref, f32[1]{0:T(128)S(6)} %copy.10.cen_ref, f32[1]{0:T(128)S(6)} %copy.11.rad_ref), custom_call_target="tpu_custom_call" | custom-call | flops 19327352832 | bytes 18874368 | tf_op jit(solution)/shard_map/chebyshev_filter/pallas_call | solution.py:301
  133.4 1.9 %copy.12 = f32[512,256]{1,0:T(8,128)} copy(f32[512,256]{1,0:T(8,128)} %chebyshev_filter.1) | data formatting | bytes 1048576

commit v2 on v1

v2 whole, which is shorter than its diff:
```python
import functools

import jax
import jax.numpy as jnp
from jax import lax
from jax.experimental import pallas as pl
from jax.experimental.pallas import tpu as pltpu
from jax.sharding import PartitionSpec as P

MESH = pl.DeviceIdType.MESH
F32 = jnp.float32
BF16 = jnp.bfloat16
BLK = 256
NT = 144
PIECE = 512
K = 256
CHUNKS = (64, 64, 64, 64)
NCH = len(CHUNKS)
STAGES = 2 * NCH
Q = CHUNKS + CHUNKS
QMAX = max(CHUNKS)
OFF = tuple(sum(Q[:k]) for k in range(STAGES))
GROUPS = 80
UNROLL = 16
PARTS = 8
SLOTS = 4
BY_X = (0, 1, 2, 3)
DIRECT = ()
CORNER = ()
X_FIRST = (6, 7)
ORDER = (
    ("turn", 0), ("turn", 1), ("turn", 2), ("ring", 0), ("turn", 3), ("far", 0), ("ring", 1), ("turn", 4),
    ("last", 0), ("turn", 5), ("own", 2), ("turn", 6), ("far", 1), ("far_ring", 0), ("far_last", 0),
    ("last", 1), ("own", 3), ("turn", 7), ("ring", 2), ("split", 0), ("mul", 0, 0, 2), ("far_ring", 1),
    ("mul", 0, 2, 4), ("far_last", 1), ("far", 2), ("mul", 0, 4, 5), ("start", 0), ("last", 2), ("split", 1),
    ("ring", 3), ("mul", 1, 0, 2), ("pass0", 0), ("far_ring", 2), ("mul", 1, 2, 3), ("last", 3), ("pass1", 0),
    ("mul", 1, 3, 4), ("far_last", 2), ("mul", 1, 4, 5), ("start", 1), ("cross", 0), ("far", 3), ("split", 2),
    ("mul", 2, 0, 3), ("pass0", 1), ("end", 0), ("own", 4), ("far_ring", 3), ("pass1", 1), ("mul", 2, 3, 4),
    ("far_last", 3), ("mul", 2, 4, 5), ("start", 2), ("cross", 1), ("split", 3), ("ring", 4),
    ("mul", 3, 0, 1), ("far", 4), ("mul", 3, 1, 3), ("pass0", 2), ("end", 1), ("pass1", 2), ("own", 5),
    ("mul", 3, 3, 5), ("start", 3), ("far_ring", 4), ("cross", 2), ("ring", 5), ("far", 5), ("last", 4),
    ("far_last", 4), ("pass0", 3), ("end", 2), ("own", 6), ("split", 4), ("mul", 4, 0, 1), ("pass1", 3),
    ("mul", 4, 1, 2), ("far_ring", 5), ("cross", 3), ("last", 5), ("mul", 4, 2, 4), ("far", 6),
    ("mul", 4, 4, 5), ("start", 4), ("far_last", 5), ("ring", 6), ("end", 3), ("own", 7), ("split", 5),
    ("mul", 5, 0, 1), ("far_ring", 6), ("mul", 5, 1, 2), ("last", 6), ("mul", 5, 2, 3), ("pass0", 4),
    ("mul", 5, 3, 4), ("far", 7), ("mul", 5, 4, 5), ("start", 5), ("far_last", 6), ("pass1", 4), ("ring", 7),
    ("cross", 4), ("split", 6), ("far_ring", 7), ("pass0", 5), ("mul", 6, 0, 2), ("pass1", 5), ("last", 7),
    ("mul", 6, 2, 3), ("far_last", 7), ("mul", 6, 3, 5), ("start", 6), ("split", 7), ("mul", 7, 0, 5),
    ("start", 7), ("first", 6), ("cross", 5), ("cross", 6), ("end", 4), ("cross", 7), ("first", 7),
    ("end", 5), ("pass1", 6), ("pass1", 7), ("end", 6), ("end", 7),
)


def filter_kernel(
    x_ref, t_hbm, rows_ref, cols_ref, live_ref, cen_ref, rad_ref, o_ref,
    tiles, gath, vals, sums, part, got_a, got_n, got_x, got_f, x_v, x_t, o_t, ivec, idx,
    x_sem, t_sem, i_sem, g_send, g_recv, r_send, r_recv,
):
    row = lax.axis_index("row")
    col = lax.axis_index("col")
    xl, z = row // 4, row % 4
    xh, y, core = col // 8, (col // 2) % 4, col % 2

    def dev(xh_, xl_, y_, z_, core_):
        return (xl_ * 4 + z_, xh_ * 8 + y_ * 2 + core_)

    up, down = dev(xh, xl, (y + 1) % 4, z, core), dev(xh, xl, (y + 3) % 4, z, core)
    zup, zdown = dev(xh, xl, y, (z + 1) % 4, core), dev(xh, xl, y, (z + 3) % 4, core)
    sib = dev(xh, xl, y, z, 1 - core)
    far = dev(1 - xh, xl, y, z, core)
    near = dev(xh, 1 - xl, y, z, core)
    corner_up, corner_down = dev(xh, 1 - xl, y, (z + 1) % 4, core), dev(xh, 1 - xl, y, (z + 3) % 4, core)
    opposite, far_opposite = dev(xh, xl, (y + 2) % 4, z, core), dev(1 - xh, xl, (y + 2) % 4, z, core)
    far_up, far_down = dev(1 - xh, xl, (y + 1) % 4, z, core), dev(1 - xh, xl, (y + 3) % 4, z, core)

    x_copy = pltpu.make_async_copy(x_ref, x_v, x_sem)
    x_copy.start()
    barrier = pltpu.get_barrier_semaphore()
    others = (up, down, zup, zdown, sib, far, near)
    if CORNER:
        others += (corner_up, corner_down)
    if DIRECT:
        others += (opposite, far_opposite, far_up, far_down)
    for other in others:
        pl.semaphore_signal(barrier, inc=1, device_id=other, device_id_type=MESH)

    per = NT // PARTS

    def tile_copy(i):
        span = pl.ds(i * per, per)
        return pltpu.make_async_copy(t_hbm.at[span], tiles.at[span], t_sem.at[i])

    for i in range(PARTS):
        tile_copy(i).start()

    def send(src, dst, ssem, rsem, to):
        pltpu.make_async_remote_copy(
            src_ref=src, dst_ref=dst, send_sem=ssem, recv_sem=rsem, device_id=to, device_id_type=MESH
        ).start()

    def wait_recv(ref, sem):
        pltpu.make_async_remote_copy(
            src_ref=ref, dst_ref=ref, send_sem=g_send, recv_sem=sem, device_id=sib, device_id_type=MESH
        ).wait_recv()

    def wait_send(ref, sem):
        pltpu.make_async_remote_copy(
            src_ref=ref, dst_ref=ref, send_sem=sem, recv_sem=g_recv.at[0, 0], device_id=sib, device_id_type=MESH
        ).wait_send()

    def rows(ref, start, count):
        return ref.at[pl.ds(start if isinstance(start, int) else pl.multiple_of(start, 16), count)]

    def piece(k, core_, xh_, y_):
        return rows(gath, 16 * OFF[k] + (core_ * 8 + xh_ * 4 + y_) * Q[k], Q[k])

    def halves(k):
        return pl.ds(0, Q[k] // 2), pl.ds(Q[k] // 2, Q[k] // 2)

    S_L, S_R, S_X, S_Y2, S_XL, S_XR, S_X2, S_SIB = range(8)

    def to_sib(k, ref):
        send(ref, ref, g_send, g_recv.at[k, S_SIB], sib)

    def gather_own(k):
        own = piece(k, core, xh, y)
        send(own, own, g_send, g_recv.at[k, S_L], up)
        send(own, own, g_send, g_recv.at[k, S_R], down)
        send(own, own, g_send, g_recv.at[k, S_X], far)
        to_sib(k, own)
        if k in DIRECT:
            send(own, own, g_send, g_recv.at[k, S_Y2], opposite)
            send(own, own, g_send, g_recv.at[k, S_XL], far_up)
            send(own, own, g_send, g_recv.at[k, S_XR], far_down)
            send(own, own, g_send, g_recv.at[k, S_X2], far_opposite)

    def gather_far(k):
        opp = piece(k, core, 1 - xh, y)
        wait_recv(opp, g_recv.at[k, S_X])
        if k not in DIRECT:
            send(opp, opp, g_send, g_recv.at[k, S_XL], up)
            send(opp, opp, g_send, g_recv.at[k, S_XR], down)
        to_sib(k, opp)

    def gather_ring(k):
        left, right = piece(k, core, xh, (y + 3) % 4), piece(k, core, xh, (y + 1) % 4)
        lo_half, hi_half = halves(k)
        wait_recv(left, g_recv.at[k, S_L])
        if k not in DIRECT:
            send(left.at[lo_half], left.at[lo_half], g_send, g_recv.at[k, S_Y2], up)
        wait_recv(right, g_recv.at[k, S_R])
        if k not in DIRECT:
            send(right.at[hi_half], right.at[hi_half], g_send, g_recv.at[k, S_Y2], down)
        to_sib(k, left)
        to_sib(k, right)

    def gather_far_ring(k):
        left, right = piece(k, core, 1 - xh, (y + 3) % 4), piece(k, core, 1 - xh, (y + 1) % 4)
        lo_half, hi_half = halves(k)
        wait_recv(left, g_recv.at[k, S_XL])
        wait_recv(right, g_recv.at[k, S_XR])
        if k not in BY_X and k not in DIRECT:
            send(left.at[lo_half], left.at[lo_half], g_send, g_recv.at[k, S_X2], up)
            send(right.at[hi_half], right.at[hi_half], g_send, g_recv.at[k, S_X2], down)
        to_sib(k, left)
        to_sib(k, right)

    def gather_last(k):
        mine = piece(k, core, xh, (y + 2) % 4)
        wait_recv(mine, g_recv.at[k, S_Y2])
        to_sib(k, mine)
        if k in BY_X:
            send(mine, mine, g_send, g_recv.at[k, S_X2], far)

    def gather_far_last(k):
        other = piece(k, core, 1 - xh, (y + 2) % 4)
        wait_recv(other, g_recv.at[k, S_X2])
        to_sib(k, other)

    def split(k):
        q = Q[k]
        wait_recv(rows(gath, 16 * OFF[k] + (1 - core) * 8 * q, 8 * q), g_recv.at[k, S_SIB])
        for core_ in range(2):
            for m in range(8):
                block = rows(gath, 16 * OFF[k] + (core_ * 8 + m) * q, q)[...]
                high = block.astype(BF16)
                low = (block - high.astype(F32)).astype(BF16)
                for t in range(2):
                    j = (2 * m + core_) * 2 + t
                    vals[j, 0:q] = high[:, t * BLK : (t + 1) * BLK]
                    vals[j, q : 2 * q] = low[:, t * BLK : (t + 1) * BLK]

    R_A, R_N, R_X = 0, 2, 4
    sides = (1 - xl, xl)

    def part_at(k, xl_, z_):
        return rows(part, (k % SLOTS) * 8 * QMAX + (xl_ * 4 + z_) * Q[k], Q[k])

    def got_a_at(k, g, side, count=1):
        return rows(got_a, 2 * OFF[k] + (g * 2 + side) * (Q[k] // 2), count * (Q[k] // 2))

    def got_n_at(k, g, side, count=1):
        return rows(got_n, 4 * OFF[k] + (g * 2 + side) * Q[k], count * Q[k])

    def multiply(k, lo, hi):
        q = Q[k]

        @pl.loop(lo, hi)
        def _(i):
            for u in range(UNROLL):
                g = i * UNROLL + u
                p0, p1 = idx[0, 2 * g], idx[0, 2 * g + 1]
                c0, c1 = idx[1, 2 * g], idx[1, 2 * g + 1]
                d = jnp.dot(vals[c0, 0 : 2 * q], tiles[p0], preferred_element_type=F32) + jnp.dot(
                    vals[c1, 0 : 2 * q], tiles[p1], preferred_element_type=F32
                )
                keep = idx[2, g].astype(F32)
                sums[g + 1, 0:q] = sums[g, 0:q] * keep + (d[:q] + d[q:])

    def send_n(k, g, half_up, half_down):
        ssem = r_send.at[k % SLOTS]
        n_up, n_down = part_at(k, sides[g], (z + 1) % 4), part_at(k, sides[g], (z + 3) % 4)
        to_up, to_down = (corner_up, corner_down) if k in CORNER and g == 0 else (zup, zdown)
        send(n_up.at[half_up], got_n_at(k, g, 0).at[half_up], ssem, r_recv.at[k, R_N + g], to_up)
        send(n_down.at[half_down], got_n_at(k, g, 1).at[half_down], ssem, r_recv.at[k, R_N + g], to_down)

    def send_a(k, g):
        ssem = r_send.at[k % SLOTS]
        lo_half, hi_half = halves(k)
        a = part_at(k, sides[g], (z + 2) % 4)
        send(a.at[lo_half], got_a_at(k, g, 0), ssem, r_recv.at[k, R_A + g], zup)
        send(a.at[hi_half], got_a_at(k, g, 1), ssem, r_recv.at[k, R_A + g], zdown)

    def reduce_start(k):
        q = Q[k]
        lo_half, hi_half = halves(k)
        if k >= SLOTS:
            wait_send(rows(part, 0, 7 * Q[k - SLOTS]), r_send.at[k % SLOTS])
        base = (k % SLOTS) * 8 * QMAX
        for i in range(16):
            at = base + (i // 2) * q
            part[at : at + q, (i % 2) * BLK : (i % 2 + 1) * BLK] = sums[idx[3, i], 0:q]
        if k in X_FIRST:
            a = part_at(k, 1 - xl, (z + 2) % 4)
            send(a, rows(got_f, OFF[k], q), r_send.at[k % SLOTS], r_recv.at[k, R_A], near)
            send_n(k, 0, pl.ds(0, q), pl.ds(0, q))
        else:
            send_a(k, 0)
            send_a(k, 1)
            send_n(k, 0, hi_half, lo_half)
        if k in CORNER:
            send(part_at(k, 1 - xl, z), rows(got_x, OFF[k], q), r_send.at[k % SLOTS], r_recv.at[k, R_X], near)

    def reduce_first(k):
        lo_half, hi_half = halves(k)
        got = rows(got_f, OFF[k], Q[k])
        wait_recv(got, r_recv.at[k, R_A])
        a = part_at(k, xl, (z + 2) % 4)
        a[...] = a[...] + got[...]
        send_a(k, 1)
        send_n(k, 1, hi_half, lo_half)

    def reduce_pass(k, g):
        h = Q[k] // 2
        lo_half, hi_half = halves(k)
        wait_recv(got_a_at(k, g, 0, 2), r_recv.at[k, R_A + g])
        n_up, n_down = part_at(k, sides[g], (z + 1) % 4), part_at(k, sides[g], (z + 3) % 4)
        n_up[0:h] = n_up[0:h] + got_a_at(k, g, 0)[...]
        n_down[h : 2 * h] = n_down[h : 2 * h] + got_a_at(k, g, 1)[...]
        send_n(k, g, lo_half, hi_half)
        if g == 0:
            send_n(k, 1, hi_half, lo_half)

    def reduce_two(k):
        wait_recv(got_n_at(k, 0, 0, 2), r_recv.at[k, R_N])
        mine = part_at(k, 1 - xl, z)
        mine[...] = mine[...] + got_n_at(k, 0, 0)[...] + got_n_at(k, 0, 1)[...]
        send(mine, rows(got_x, OFF[k], Q[k]), r_send.at[k % SLOTS], r_recv.at[k, R_X], near)

    def reduce_end(k):
        got = rows(got_x, OFF[k], Q[k])
        wait_recv(got_n_at(k, 1, 0, 2), r_recv.at[k, R_N + 1])
        wait_recv(got, r_recv.at[k, R_X])
        mine = part_at(k, xl, z)
        total = mine[...] + got_n_at(k, 1, 0)[...] + got_n_at(k, 1, 1)[...] + got[...]
        if k in CORNER:
            wait_recv(got_n_at(k, 0, 0, 2), r_recv.at[k, R_N])
            total = total + got_n_at(k, 0, 0)[...] + got_n_at(k, 0, 1)[...]
        center, radius = cen_ref[0], rad_ref[0]
        cols_at = pl.ds(OFF[k % NCH], Q[k])
        start = x_t[cols_at]
        if k < NCH:
            piece(k + NCH, core, xh, y)[...] = (total - center * start) / radius
        else:
            first = piece(k, core, xh, y)[...]
            o_t[cols_at] = 2.0 * (total - center * first) / radius - start

    x_copy.wait()
    x_t[...] = x_v[...].T
    for j in range(NCH):
        piece(j, core, xh, y)[...] = x_t[OFF[j] : OFF[j] + Q[j]]
    pl.semaphore_wait(barrier, len(others))

    gather_own(0)
    gather_own(1)

    ivec[...] = jnp.full(ivec.shape, 99, jnp.int32)
    ivec[0:1, 0:NT] = rows_ref[...]
    ivec[1:2, 0:NT] = cols_ref[...]
    lanes = lax.broadcasted_iota(jnp.int32, (1, 256), 1)
    row_of = jnp.where(lanes < live_ref[0], ivec[0:1], 99)
    row_l = jnp.broadcast_to(row_of, (256, 256))
    row_s = row_l.T
    col_s = jnp.broadcast_to(ivec[1:2], (256, 256)).T
    li = lax.broadcasted_iota(jnp.int32, (256, 256), 1)
    si = lax.broadcasted_iota(jnp.int32, (256, 256), 0)

    def count(mask, value=1, axis=1):
        return jnp.sum(jnp.where(mask, value, 0), axis=axis, keepdims=True)

    within = count((row_l == row_s) & (li < si))
    pairs = (count(row_s == li, axis=0) + 1) >> 1
    before = count(li < row_s, pairs)
    pairs_s = count(li == row_s, pairs)
    live = row_s < 16
    place = live & (2 * before + within == li)
    leads = live & (within == 0)
    ivec[0:1] = count(place, si, 0)
    ivec[1:2] = count(place, col_s - 32, 0) + 32
    ivec[2:3] = 1 - count(leads & (before == li), 1, 0)
    ivec[3:4] = count(leads & (row_s <= li), pairs_s, 0)
    to_smem = pltpu.make_async_copy(ivec, idx, i_sem)
    to_smem.start()

    def turn(i):
        tile_copy(i).wait()

        @pl.loop(0, per // 6)
        def _(s):
            for u in range(6):
                at = i * per + s * 6 + u
                tiles[at] = tiles[at].T

    vals[32] = jnp.zeros((2 * QMAX, BLK), BF16)
    sums[0] = jnp.zeros((QMAX, BLK), F32)

    step = {
        "own": gather_own, "far": gather_far, "ring": gather_ring, "far_ring": gather_far_ring,
        "last": gather_last, "far_last": gather_far_last, "split": split, "start": reduce_start,
        "first": reduce_first, "pass0": lambda k: reduce_pass(k, 0), "pass1": lambda k: reduce_pass(k, 1),
        "cross": reduce_two, "end": reduce_end, "turn": turn,
    }
    multiplied = 0
    for name, k, *span in ORDER:
        if name == "mul":
            if multiplied == 0 and k == 0:
                to_smem.wait()
                multiplied = 1
            multiply(k, *span)
        else:
            step[name](k)

    wait_send(rows(gath, 0, 15 * 2 * K), g_send)
    for k in range(STAGES - SLOTS, STAGES):
        wait_send(rows(part, 0, 7 * Q[k]), r_send.at[k % SLOTS])
    o_ref[...] = o_t[...].T


def local(start_basis, affinity_tiles, tile_rows, tile_cols, live_tiles, filter_center, filter_radius):
    vmem = pl.BlockSpec(memory_space=pltpu.VMEM)
    smem = pl.BlockSpec(memory_space=pltpu.SMEM)
    return pl.pallas_call(
        filter_kernel,
        name="chebyshev_filter",
        out_shape=jax.ShapeDtypeStruct((PIECE, K), F32),
        in_specs=[pl.BlockSpec(memory_space=pl.ANY), pl.BlockSpec(memory_space=pl.ANY), vmem, vmem, smem, smem, smem],
        out_specs=vmem,
        scratch_shapes=[
            pltpu.VMEM((NT, BLK, BLK), BF16),
            pltpu.VMEM((16 * 2 * K, PIECE), F32),
            pltpu.VMEM((33, 2 * QMAX, BLK), BF16),
            pltpu.VMEM((GROUPS + 1, QMAX, BLK), F32),
            pltpu.VMEM((SLOTS * 8 * QMAX, PIECE), F32),
            pltpu.VMEM((2 * 2 * K, PIECE), F32),
            pltpu.VMEM((4 * 2 * K, PIECE), F32),
            pltpu.VMEM((2 * K, PIECE), F32),
            pltpu.VMEM((2 * K, PIECE), F32),
            pltpu.VMEM((PIECE, K), F32),
            pltpu.VMEM((K, PIECE), F32),
            pltpu.VMEM((K, PIECE), F32),
            pltpu.VMEM((8, 256), jnp.int32),
            pltpu.SMEM((8, 256), jnp.int32),
            pltpu.SemaphoreType.DMA,
            pltpu.SemaphoreType.DMA((PARTS,)),
            pltpu.SemaphoreType.DMA,
            pltpu.SemaphoreType.DMA,
            pltpu.SemaphoreType.DMA((STAGES, 8)),
            pltpu.SemaphoreType.DMA((SLOTS,)),
            pltpu.SemaphoreType.DMA((STAGES, 5)),
        ],
        compiler_params=pltpu.CompilerParams(
            collective_id=0, has_side_effects=True, vmem_limit_bytes=60 * 2**20
        ),
        cost_estimate=pl.CostEstimate(
            flops=4 * NT * BLK * BLK * K * 2, bytes_accessed=NT * BLK * BLK * 2, transcendentals=0
        ),
    )(
        start_basis, affinity_tiles, tile_rows.reshape(1, NT), tile_cols.reshape(1, NT),
        live_tiles, filter_center, filter_radius,
    )


def solution(mesh):
    return jax.shard_map(
        local,
        mesh=mesh,
        in_specs=(
            P(("row", "col"), None),
            P(("row", "col"), None, None),
            P(("row", "col")),
            P(("row", "col")),
            P(("row", "col")),
            P(),
            P(),
        ),
        out_specs=P(("row", "col"), None),
        check_vma=False,
    )
```

time: 136 us -> 109 us (0.80)
  Pallas kernels: 131 us -> 105 us
    pallas_call x1, Pallas kernels: 131 us -> 105 us  [local(): pl.pallas_call(filter_kernel, name='chebyshev_filter', out_shape=jax.Shap...]
where the time goes in v2:
time: 109 us
  Pallas kernels  105 us (96%)
  between operations  1.95 us (2%)
  local copies, waits for them, and re-layouts  1.87 us (2%)
    pallas_call x1, Pallas kernels, local(): pl.pallas_call(filter_kernel, name='chebyshev_filter', out_shape=jax.Shap...  105 us

profile of v2, /device:TPU:0, one launch (start us, length us, event | category | flops | bytes accessed | tf_op | source)
XLA Modules:
  0.0 108.7 jit_solution(8380878849871808863)
XLA Ops:
  1.9 104.9 %chebyshev_filter.1 = f32[512,256]{1,0:T(8,128)} custom-call(f32[512,256]{1,0:T(8,128)} %x_ref.1, bf16[144,256,256]{2,1,0:T(8,128)(2,1)} %t_hbm.1, s32[1,144]{1,0:T(1,128)} %bitcast.2, s32[1,144]{1,0:T(1,128)} %bitcast.3, s32[1]{0:T(128)S(6)} %copy.9.live_ref, f32[1]{0:T(128)S(6)} %copy.10.cen_ref, f32[1]{0:T(128)S(6)} %copy.11.rad_ref), custom_call_target="tpu_custom_call" | custom-call | flops 19327352832 | bytes 18874368 | tf_op jit(solution)/shard_map/chebyshev_filter/pallas_call | solution.py:372
  106.8 1.9 %copy.12 = f32[512,256]{1,0:T(8,128)} copy(f32[512,256]{1,0:T(8,128)} %chebyshev_filter.1) | data formatting | bytes 1048576

commit v3 on v2

--- a/solution.py
+++ b/solution.py
@@ -14,7 +14,7 @@
 NT = 144
 PIECE = 512
 K = 256
-CHUNKS = (64, 64, 64, 64)
+CHUNKS = (48, 48, 48, 48, 64)
 NCH = len(CHUNKS)
 STAGES = 2 * NCH
 Q = CHUNKS + CHUNKS
@@ -24,30 +24,35 @@
 UNROLL = 16
 PARTS = 8
 SLOTS = 4
-BY_X = (0, 1, 2, 3)
+BY_X = (0, 1, 2, 3, 4)
 DIRECT = ()
 CORNER = ()
-X_FIRST = (6, 7)
+X_FIRST = (8, 9)
 ORDER = (
-    ("turn", 0), ("turn", 1), ("turn", 2), ("ring", 0), ("turn", 3), ("far", 0), ("ring", 1), ("turn", 4),
-    ("last", 0), ("turn", 5), ("own", 2), ("turn", 6), ("far", 1), ("far_ring", 0), ("far_last", 0),
-    ("last", 1), ("own", 3), ("turn", 7), ("ring", 2), ("split", 0), ("mul", 0, 0, 2), ("far_ring", 1),
-    ("mul", 0, 2, 4), ("far_last", 1), ("far", 2), ("mul", 0, 4, 5), ("start", 0), ("last", 2), ("split", 1),
-    ("ring", 3), ("mul", 1, 0, 2), ("pass0", 0), ("far_ring", 2), ("mul", 1, 2, 3), ("last", 3), ("pass1", 0),
-    ("mul", 1, 3, 4), ("far_last", 2), ("mul", 1, 4, 5), ("start", 1), ("cross", 0), ("far", 3), ("split", 2),
-    ("mul", 2, 0, 3), ("pass0", 1), ("end", 0), ("own", 4), ("far_ring", 3), ("pass1", 1), ("mul", 2, 3, 4),
-    ("far_last", 3), ("mul", 2, 4, 5), ("start", 2), ("cross", 1), ("split", 3), ("ring", 4),
-    ("mul", 3, 0, 1), ("far", 4), ("mul", 3, 1, 3), ("pass0", 2), ("end", 1), ("pass1", 2), ("own", 5),
-    ("mul", 3, 3, 5), ("start", 3), ("far_ring", 4), ("cross", 2), ("ring", 5), ("far", 5), ("last", 4),
-    ("far_last", 4), ("pass0", 3), ("end", 2), ("own", 6), ("split", 4), ("mul", 4, 0, 1), ("pass1", 3),
-    ("mul", 4, 1, 2), ("far_ring", 5), ("cross", 3), ("last", 5), ("mul", 4, 2, 4), ("far", 6),
-    ("mul", 4, 4, 5), ("start", 4), ("far_last", 5), ("ring", 6), ("end", 3), ("own", 7), ("split", 5),
-    ("mul", 5, 0, 1), ("far_ring", 6), ("mul", 5, 1, 2), ("last", 6), ("mul", 5, 2, 3), ("pass0", 4),
-    ("mul", 5, 3, 4), ("far", 7), ("mul", 5, 4, 5), ("start", 5), ("far_last", 6), ("pass1", 4), ("ring", 7),
-    ("cross", 4), ("split", 6), ("far_ring", 7), ("pass0", 5), ("mul", 6, 0, 2), ("pass1", 5), ("last", 7),
-    ("mul", 6, 2, 3), ("far_last", 7), ("mul", 6, 3, 5), ("start", 6), ("split", 7), ("mul", 7, 0, 5),
-    ("start", 7), ("first", 6), ("cross", 5), ("cross", 6), ("end", 4), ("cross", 7), ("first", 7),
-    ("end", 5), ("pass1", 6), ("pass1", 7), ("end", 6), ("end", 7),
+    ("turn", 0), ("turn", 1), ("ring", 0), ("far", 0), ("turn", 2), ("own", 2), ("turn", 3), ("turn", 4),
+    ("ring", 1), ("last", 0), ("turn", 5), ("far_ring", 0), ("own", 3), ("far", 1), ("turn", 6), ("turn", 7),
+    ("far_last", 0), ("last", 1), ("ring", 2), ("own", 4), ("split", 0), ("mul", 0, 0, 1), ("far", 2),
+    ("mul", 0, 1, 2), ("ring", 3), ("far", 3), ("mul", 0, 2, 4), ("far_ring", 1), ("far_last", 1),
+    ("last", 2), ("mul", 0, 4, 5), ("start", 0), ("split", 1), ("mul", 1, 0, 3), ("ring", 4), ("far_ring", 2),
+    ("far", 4), ("pass0", 0), ("mul", 1, 3, 4), ("last", 3), ("far_last", 2), ("mul", 1, 4, 5), ("start", 1),
+    ("split", 2), ("pass1", 0), ("mul", 2, 0, 1), ("cross", 0), ("last", 4), ("mul", 2, 1, 2),
+    ("far_ring", 3), ("mul", 2, 2, 3), ("far_last", 3), ("pass0", 1), ("mul", 2, 3, 5), ("start", 2),
+    ("split", 3), ("end", 0), ("own", 5), ("mul", 3, 0, 1), ("pass1", 1), ("cross", 1), ("far_ring", 4),
+    ("mul", 3, 1, 3), ("pass0", 2), ("mul", 3, 3, 4), ("far_last", 4), ("mul", 3, 4, 5), ("start", 3),
+    ("far", 5), ("split", 4), ("mul", 4, 0, 1), ("end", 1), ("own", 6), ("cross", 2), ("pass1", 2),
+    ("ring", 5), ("mul", 4, 1, 3), ("pass0", 3), ("mul", 4, 3, 4), ("far_ring", 5), ("pass1", 3),
+    ("mul", 4, 4, 5), ("start", 4), ("far", 6), ("last", 5), ("cross", 3), ("ring", 6), ("far_last", 5),
+    ("end", 2), ("own", 7), ("split", 5), ("mul", 5, 0, 1), ("pass0", 4), ("far_ring", 6), ("mul", 5, 1, 2),
+    ("end", 3), ("own", 8), ("mul", 5, 2, 3), ("last", 6), ("mul", 5, 3, 4), ("far", 7), ("cross", 4),
+    ("far_last", 6), ("ring", 7), ("pass1", 4), ("mul", 5, 4, 5), ("start", 5), ("split", 6), ("far", 8),
+    ("mul", 6, 0, 2), ("far_ring", 7), ("mul", 6, 2, 3), ("end", 4), ("own", 9), ("pass0", 5), ("last", 7),
+    ("mul", 6, 3, 4), ("far_ring", 8), ("ring", 8), ("pass1", 5), ("far_last", 7), ("mul", 6, 4, 5),
+    ("start", 6), ("split", 7), ("cross", 5), ("mul", 7, 0, 1), ("far", 9), ("mul", 7, 1, 3), ("far_last", 8),
+    ("last", 8), ("pass0", 6), ("mul", 7, 3, 4), ("ring", 9), ("mul", 7, 4, 5), ("start", 7), ("pass1", 6),
+    ("end", 5), ("split", 8), ("far_ring", 9), ("mul", 8, 0, 4), ("last", 9), ("pass0", 7), ("cross", 6),
+    ("pass1", 7), ("far_last", 9), ("mul", 8, 4, 5), ("start", 8), ("split", 9), ("mul", 9, 0, 5),
+    ("start", 9), ("first", 8), ("cross", 7), ("first", 9), ("cross", 8), ("cross", 9), ("end", 7),
+    ("pass1", 8), ("pass1", 9), ("end", 8), ("end", 6), ("end", 9),
 )
 
 

time: 109 us -> 107 us (0.982)
  Pallas kernels: 105 us -> 103 us
    pallas_call x1, Pallas kernels: 105 us -> 103 us  [local(): pl.pallas_call(filter_kernel, name='chebyshev_filter', out_shape=jax.Shap...]
where the time goes in v3:
time: 107 us
  Pallas kernels  103 us (96%)
  between operations  1.95 us (2%)
  local copies, waits for them, and re-layouts  1.87 us (2%)
    pallas_call x1, Pallas kernels, local(): pl.pallas_call(filter_kernel, name='chebyshev_filter', out_shape=jax.Shap...  103 us

profile of v3, /device:TPU:0, one launch (start us, length us, event | category | flops | bytes accessed | tf_op | source)
XLA Modules:
  0.0 107.1 jit_solution(8868822154354424249)
XLA Ops:
  1.9 103.3 %chebyshev_filter.1 = f32[512,256]{1,0:T(8,128)} custom-call(f32[512,256]{1,0:T(8,128)} %x_ref.1, bf16[144,256,256]{2,1,0:T(8,128)(2,1)} %t_hbm.1, s32[1,144]{1,0:T(1,128)} %bitcast.2, s32[1,144]{1,0:T(1,128)} %bitcast.3, s32[1]{0:T(128)S(6)} %copy.9.live_ref, f32[1]{0:T(128)S(6)} %copy.10.cen_ref, f32[1]{0:T(128)S(6)} %copy.11.rad_ref), custom_call_target="tpu_custom_call" | custom-call | flops 19327352832 | bytes 18874368 | tf_op jit(solution)/shard_map/chebyshev_filter/pallas_call | solution.py:377
  105.3 1.9 %copy.12 = f32[512,256]{1,0:T(8,128)} copy(f32[512,256]{1,0:T(8,128)} %chebyshev_filter.1) | data formatting | bytes 1048576

commit v4 on v2

--- a/solution.py
+++ b/solution.py
@@ -14,7 +14,7 @@
 NT = 144
 PIECE = 512
 K = 256
-CHUNKS = (64, 64, 64, 64)
+CHUNKS = (48, 48, 48, 64, 48)
 NCH = len(CHUNKS)
 STAGES = 2 * NCH
 Q = CHUNKS + CHUNKS
@@ -24,30 +24,36 @@
 UNROLL = 16
 PARTS = 8
 SLOTS = 4
-BY_X = (0, 1, 2, 3)
+BY_X = (0, 1, 2, 3, 4)
 DIRECT = ()
 CORNER = ()
-X_FIRST = (6, 7)
+X_FIRST = (8, 9)
 ORDER = (
-    ("turn", 0), ("turn", 1), ("turn", 2), ("ring", 0), ("turn", 3), ("far", 0), ("ring", 1), ("turn", 4),
-    ("last", 0), ("turn", 5), ("own", 2), ("turn", 6), ("far", 1), ("far_ring", 0), ("far_last", 0),
-    ("last", 1), ("own", 3), ("turn", 7), ("ring", 2), ("split", 0), ("mul", 0, 0, 2), ("far_ring", 1),
-    ("mul", 0, 2, 4), ("far_last", 1), ("far", 2), ("mul", 0, 4, 5), ("start", 0), ("last", 2), ("split", 1),
-    ("ring", 3), ("mul", 1, 0, 2), ("pass0", 0), ("far_ring", 2), ("mul", 1, 2, 3), ("last", 3), ("pass1", 0),
-    ("mul", 1, 3, 4), ("far_last", 2), ("mul", 1, 4, 5), ("start", 1), ("cross", 0), ("far", 3), ("split", 2),
-    ("mul", 2, 0, 3), ("pass0", 1), ("end", 0), ("own", 4), ("far_ring", 3), ("pass1", 1), ("mul", 2, 3, 4),
-    ("far_last", 3), ("mul", 2, 4, 5), ("start", 2), ("cross", 1), ("split", 3), ("ring", 4),
-    ("mul", 3, 0, 1), ("far", 4), ("mul", 3, 1, 3), ("pass0", 2), ("end", 1), ("pass1", 2), ("own", 5),
-    ("mul", 3, 3, 5), ("start", 3), ("far_ring", 4), ("cross", 2), ("ring", 5), ("far", 5), ("last", 4),
-    ("far_last", 4), ("pass0", 3), ("end", 2), ("own", 6), ("split", 4), ("mul", 4, 0, 1), ("pass1", 3),
-    ("mul", 4, 1, 2), ("far_ring", 5), ("cross", 3), ("last", 5), ("mul", 4, 2, 4), ("far", 6),
-    ("mul", 4, 4, 5), ("start", 4), ("far_last", 5), ("ring", 6), ("end", 3), ("own", 7), ("split", 5),
-    ("mul", 5, 0, 1), ("far_ring", 6), ("mul", 5, 1, 2), ("last", 6), ("mul", 5, 2, 3), ("pass0", 4),
-    ("mul", 5, 3, 4), ("far", 7), ("mul", 5, 4, 5), ("start", 5), ("far_last", 6), ("pass1", 4), ("ring", 7),
-    ("cross", 4), ("split", 6), ("far_ring", 7), ("pass0", 5), ("mul", 6, 0, 2), ("pass1", 5), ("last", 7),
-    ("mul", 6, 2, 3), ("far_last", 7), ("mul", 6, 3, 5), ("start", 6), ("split", 7), ("mul", 7, 0, 5),
-    ("start", 7), ("first", 6), ("cross", 5), ("cross", 6), ("end", 4), ("cross", 7), ("first", 7),
-    ("end", 5), ("pass1", 6), ("pass1", 7), ("end", 6), ("end", 7),
+    ("turn", 0), ("turn", 1), ("ring", 0), ("turn", 2), ("own", 2), ("turn", 3), ("ring", 1), ("far", 0),
+    ("far", 1), ("turn", 4), ("last", 0), ("turn", 5), ("turn", 6), ("ring", 2), ("last", 1), ("own", 3),
+    ("far_ring", 0), ("far_last", 0), ("own", 4), ("far", 2), ("turn", 7), ("split", 0), ("mul", 0, 0, 1),
+    ("far_ring", 1), ("mul", 0, 1, 3), ("last", 2), ("far_last", 1), ("mul", 0, 3, 4), ("ring", 3),
+    ("mul", 0, 4, 5), ("start", 0), ("split", 1), ("mul", 1, 0, 2), ("far", 3), ("mul", 1, 2, 3),
+    ("far_ring", 2), ("ring", 4), ("far_last", 2), ("pass0", 0), ("far", 4), ("last", 3), ("mul", 1, 3, 5),
+    ("start", 1), ("split", 2), ("mul", 2, 0, 1), ("pass1", 0), ("cross", 0), ("mul", 2, 1, 3), ("last", 4),
+    ("far_ring", 3), ("far_last", 3), ("pass0", 1), ("mul", 2, 3, 5), ("start", 2), ("split", 3), ("end", 0),
+    ("own", 5), ("mul", 3, 0, 1), ("far_ring", 4), ("mul", 3, 1, 2), ("cross", 1), ("pass1", 1),
+    ("mul", 3, 2, 3), ("pass0", 2), ("mul", 3, 3, 4), ("far_last", 4), ("pass1", 2), ("far", 5),
+    ("mul", 3, 4, 5), ("start", 3), ("ring", 5), ("split", 4), ("cross", 2), ("end", 1), ("mul", 4, 0, 1),
+    ("own", 6), ("mul", 4, 1, 3), ("pass0", 3), ("far_ring", 5), ("mul", 4, 3, 4), ("end", 2), ("own", 7),
+    ("mul", 4, 4, 5), ("start", 4), ("last", 5), ("far", 6), ("far_last", 5), ("cross", 3), ("pass1", 3),
+    ("split", 5), ("ring", 6), ("mul", 5, 0, 1), ("ring", 7), ("pass0", 4), ("mul", 5, 1, 2), ("far_ring", 6),
+    ("pass1", 4), ("mul", 5, 2, 3), ("far", 7), ("end", 3), ("own", 8), ("mul", 5, 3, 4), ("last", 6),
+    ("last", 7), ("cross", 4), ("far_last", 6), ("mul", 5, 4, 5), ("start", 5), ("split", 6),
+    ("mul", 6, 0, 1), ("far_ring", 7), ("mul", 6, 1, 2), ("far", 8), ("mul", 6, 2, 3), ("ring", 8),
+    ("end", 4), ("own", 9), ("pass0", 5), ("mul", 6, 3, 4), ("far_last", 7), ("mul", 6, 4, 5), ("start", 6),
+    ("pass1", 5), ("split", 7), ("mul", 7, 0, 1), ("far_ring", 8), ("cross", 5), ("far", 9), ("mul", 7, 1, 2),
+    ("last", 8), ("mul", 7, 2, 3), ("ring", 9), ("pass0", 6), ("mul", 7, 3, 4), ("far_last", 8),
+    ("mul", 7, 4, 5), ("start", 7), ("split", 8), ("end", 5), ("pass1", 6), ("far_ring", 9), ("mul", 8, 0, 1),
+    ("last", 9), ("mul", 8, 1, 4), ("cross", 6), ("pass0", 7), ("far_last", 9), ("mul", 8, 4, 5),
+    ("start", 8), ("split", 9), ("mul", 9, 0, 1), ("pass1", 7), ("mul", 9, 1, 5), ("start", 9), ("first", 8),
+    ("cross", 8), ("first", 9), ("cross", 7), ("pass1", 8), ("end", 6), ("cross", 9), ("pass1", 9),
+    ("end", 8), ("end", 7), ("end", 9),
 )
 
 

time: 109 us -> 109 us (level)
  no operation moved by 1% of the time
where the time goes in v4:
time: 109 us
  Pallas kernels  105 us (96%)
  between operations  1.95 us (2%)
  local copies, waits for them, and re-layouts  1.87 us (2%)
    pallas_call x1, Pallas kernels, local(): pl.pallas_call(filter_kernel, name='chebyshev_filter', out_shape=jax.Shap...  105 us

profile of v4, /device:TPU:0, one launch (start us, length us, event | category | flops | bytes accessed | tf_op | source)
XLA Modules:
  0.0 108.5 jit_solution(13172435194633620344)
XLA Ops:
  1.9 104.7 %chebyshev_filter.1 = f32[512,256]{1,0:T(8,128)} custom-call(f32[512,256]{1,0:T(8,128)} %x_ref.1, bf16[144,256,256]{2,1,0:T(8,128)(2,1)} %t_hbm.1, s32[1,144]{1,0:T(1,128)} %bitcast.2, s32[1,144]{1,0:T(1,128)} %bitcast.3, s32[1]{0:T(128)S(6)} %copy.9.live_ref, f32[1]{0:T(128)S(6)} %copy.10.cen_ref, f32[1]{0:T(128)S(6)} %copy.11.rad_ref), custom_call_target="tpu_custom_call" | custom-call | flops 19327352832 | bytes 18874368 | tf_op jit(solution)/shard_map/chebyshev_filter/pallas_call | solution.py:378
  106.6 1.9 %copy.12 = f32[512,256]{1,0:T(8,128)} copy(f32[512,256]{1,0:T(8,128)} %chebyshev_filter.1) | data formatting | bytes 1048576
